TPU v7x, 32 devices: a whole 2x2x4 slice. The times are simulated.
32 devices in a mesh: table: 16 (over z, y, core), rep: 2 (over x).
Axes of the slice: x: 2, y: 2, z: 4, core: 2. Of those that a mesh axis runs over, the one named last changes fastest.
Arguments:
- bag_rows: int32 [32, 1024, 8], P(('table', 'rep')), may hold values from 0 to 2047
- bag_owner: int32 [32, 1024, 8], P(('table', 'rep')), may hold values from 0 to 15, all different within a row; in each aligned block of 1024 rows (0 to 1023, 1024 to 2047, ..., all dimensions but the last counted through in order) at most 768 rows name the same one
- bag_weight: float32 [32, 1024, 8], P(('table', 'rep')), may hold values from 0.25 to 2
- tables: bfloat16 [4, 32768, 128], P(None, 'table'), may hold values from -3 to 3
- returning: int32 [32], P(('table', 'rep')), may hold values 0 or 1
- home: int32 [32], P(('table', 'rep')), may hold values from 0 to 1
- entry: int32 [32], P(('table', 'rep')), may hold values from 0 to 7
- stores: bfloat16 [256, 30, 512], P(('table', 'rep')), may hold values from -6 to 6
- conv_weight: bfloat16 [4, 1536, 512], P(None, 'table'), may hold values from -0.15625 to 0.15625
- norm_gain: float32 [4, 512], replicated, may hold values from 0.1 to 1.9
Outputs:
- hidden: bfloat16 [32, 1024, 512], P(('table', 'rep'))
Inputs may be any that keep to these rules, and one draw needn't show every extreme that they name: `bag_owner`: the 8 ids of one slot name different owners. Among the slots of one device no owner is named by more than 768 ids, and in some devices' slots one owner is named by exactly 768.
All inputs are finite; a program needn't handle non-finite values. No bound on the sum of `returning` on one device may be relied on, other than what follows from the above.
Results may differ from a plain program's by a relative error of at most 0.0057.
Values may be sent and summed in bfloat16 or wider, within the bound.
No kernel may reach another device: no remote copies, remote signals or barrier semaphores. Data moves between devices by JAX's collectives and lax.ppermute only.
A program may use at most 64 MiB of HBM per device.

v0:
```python
import functools
import jax
import jax.numpy as jnp
from jax import lax
from jax.experimental import pallas as pl
from jax.experimental.pallas import tpu as pltpu
from jax.sharding import PartitionSpec as P

table_of_id = (0, 1, 2, 2, 3, 3, 3, 3)
bag_bounds = ((0, 1), (1, 2), (2, 4), (4, 8))
epsilon = 1e-05
part_ends = (0.25, 5 / 6, 1.0)
megabyte = 1024 * 1024


def prep_kernel(cuts, shard_rows, rows_ref, owner_ref, request_ref, place_ref):
    owner = owner_ref[...]
    rows = rows_ref[...]
    owners = request_ref.shape[0]
    width, slots = owner.shape
    value_bits = (len(bag_bounds) * shard_rows).bit_length()
    owner_ids = lax.broadcasted_iota(jnp.int32, (owners, slots), 0)
    lane = lax.broadcasted_iota(jnp.int32, (owners, slots), 1)
    value = jnp.zeros((owners, slots), jnp.int32)
    for k in range(width):
        named = owner[k : k + 1, :] == owner_ids
        value = jnp.where(named, rows[k : k + 1, :] + (table_of_id[k] * shard_rows + 1), value)
    present = jnp.where(value > 0, 1, 0)
    rank = present
    step = 1
    while step < slots:
        rank = rank + jnp.where(lane >= step, pltpu.roll(rank, step, 1), 0)
        step *= 2
    rank = rank - present
    place = jnp.zeros((width, slots), jnp.int32)
    for number in range(owners):
        place = jnp.where(owner == number, rank[number : number + 1, :], place)
    landing = jnp.zeros((width, slots), jnp.int32)
    for start, stop in zip(cuts[:-1], cuts[1:]):
        where = owners * start + owner * (stop - start) + place - start
        landing = jnp.where(place >= start, where, landing)
    place_ref[...] = landing
    packed = jnp.where(value > 0, ((lane - rank) << value_bits) + value, 0)
    step = 1
    level = value_bits
    while step < slots:
        moving = jnp.where(((packed >> level) & 1) == 1, packed, 0)
        packed = (packed - moving) + pltpu.roll(moving, slots - step, 1)
        step *= 2
        level += 1
    value = jnp.maximum((packed & ((1 << value_bits) - 1)) - 1, 0)
    for number in range(owners):
        request_ref[number] = value[number : number + 1, : request_ref.shape[2]]


def pass_kernel(*refs):
    pass


def tie(array, *others):
    anywhere = pl.BlockSpec(memory_space=pl.ANY)
    return pl.pallas_call(
        pass_kernel,
        out_shape=jax.ShapeDtypeStruct(array.shape, array.dtype),
        in_specs=[anywhere] * (1 + len(others)),
        out_specs=anywhere,
        input_output_aliases={0: 0},
        name="tie",
    )(array, *others)


def gather_kernel(capacity, first, index_ref, table_ref, *refs):
    out_ref, narrow, wide, picked, packed, index, index_sem, table_sems, out_sems = refs[-9:]
    owners, piece, _ = out_ref.shape
    unroll = 32 if piece % 32 == 0 else 16
    blocks = table_sems.shape[0]
    block_rows = table_ref.shape[0] // blocks
    table_copies = []
    for block in range(blocks):
        part = pl.ds(block * block_rows, block_rows)
        copy = pltpu.make_async_copy(table_ref.at[part, :], narrow.at[part, :], table_sems.at[block])
        copy.start()
        table_copies.append(copy)
    index_copy = pltpu.make_async_copy(index_ref, index, index_sem)
    index_copy.start()
    rows = 256

    for block in range(blocks):
        table_copies[block].wait()

        def widen(step, carry, block=block):
            base = pl.multiple_of(block * block_rows + step * rows, rows)
            wide[pl.ds(base, rows), :] = narrow[pl.ds(base, rows), :].astype(jnp.float32)
            return carry

        lax.fori_loop(0, block_rows // rows, widen, 0)
    index_copy.wait()
    copies = []
    for number in range(owners):
        origin = number * capacity + first

        def some_rows(block, carry, origin=origin):
            base = pl.multiple_of(block * unroll, unroll)
            picks = [index[origin + base + i] for i in range(unroll)]
            found = [wide[pl.ds(pick, 1), :] for pick in picks]
            for i in range(unroll):
                picked[pl.ds(base + i, 1), :] = found[i]
            return carry

        lax.fori_loop(0, piece // unroll, some_rows, 0)
        packed[number] = picked[...].astype(jnp.bfloat16)
        copy = pltpu.make_async_copy(packed.at[number], out_ref.at[number], out_sems.at[number])
        copy.start()
        copies.append(copy)
    for copy in copies:
        copy.wait()


def pool_slots(first, place_ref, weight_ref, piece_refs, table, picked, put):
    width, slots, lanes = picked.shape
    start = 0
    for piece_ref in piece_refs:
        count = piece_ref.shape[0]
        rows = 256

        def widen(step, carry, piece_ref=piece_ref, start=start):
            base = pl.multiple_of(step * rows, rows)
            table[pl.ds(start + base, rows), :] = piece_ref[pl.ds(base, rows), :].astype(jnp.float32)
            return carry

        lax.fori_loop(0, count // rows, widen, 0)
        start += count

    def some_slots(step, carry):
        base = pl.multiple_of(step * 8, 8)
        for k in range(width):
            picks = [place_ref[k, first + base + i] for i in range(8)]
            rows = [table[pl.ds(pick, 1), :] for pick in picks]
            for i in range(8):
                picked[k, pl.ds(base + i, 1), :] = rows[i]
        return carry

    lax.fori_loop(0, slots // 8, some_slots, 0)
    weights = jnp.transpose(weight_ref[:, first : first + slots])
    for t, (lower, upper) in enumerate(bag_bounds):
        total = picked[lower] * weights[:, lower : lower + 1]
        for k in range(lower + 1, upper):
            total = total + picked[k] * weights[:, k : k + 1]
        put(slice(t * lanes, (t + 1) * lanes), total.astype(jnp.bfloat16))


def pool_kernel(place_ref, weight_ref, *refs):
    out_ref, table, picked = refs[-3:]

    def put(columns, total):
        out_ref[:, columns] = total

    pool_slots(0, place_ref, weight_ref, refs[:-3], table, picked, put)


def stage_kernel(
    pieces, sources, place_ref, me_ref, weight_ref, carried_ref, gain_ref, pooled_ref, *refs
):
    piece_refs = refs[:pieces]
    filter_refs = refs[pieces : pieces + sources]
    out_ref, table, picked, filters, first_buf, second_buf, result = refs[pieces + sources :][:7]
    filter_sems, out_sems = refs[pieces + sources :][7:]
    slots = result.shape[0]
    layers = filters.shape[0]
    filter_copies = []
    if sources == 1:
        filter_copies.append(pltpu.make_async_copy(filter_refs[0], filters, filter_sems.at[0]))
    else:
        held, half, depth, _ = filter_refs[0].shape
        for group, filter_ref in enumerate(filter_refs):
            bits, side = block_place(group, me_ref[1])
            for number in range(filter_ref.shape[0]):
                owner = me_ref[0] ^ (4 * number + bits)
                rows = pl.ds(pl.multiple_of(owner * depth, depth), depth)
                filter_copies.append(
                    pltpu.make_async_copy(
                        filter_ref.at[number],
                        filters.at[pl.ds(side * half, half), rows, :],
                        filter_sems.at[len(filter_copies)],
                    )
                )
    for copy in filter_copies:
        copy.start()
    front = 16
    early = pooled_ref.shape[0]
    first_buf[front : front + early, :] = pooled_ref[...].astype(jnp.float32)

    def put(columns, total):
        first_buf[front + early :, columns] = total.astype(jnp.float32)

    pool_slots(early, place_ref, weight_ref, piece_refs, table, picked, put)
    for copy in filter_copies:
        copy.wait()
    offset = 0
    out_copies = []
    for layer in range(layers):
        dilation = 2**layer
        span = 2 * dilation
        source, target = (first_buf, second_buf) if layer % 2 == 0 else (second_buf, first_buf)
        source[front - span : front, :] = carried_ref[offset : offset + span, :]
        offset += span
        for begin in range(0, slots, 256):
            rows = min(256, slots - begin)
            base = front + begin
            taps = [
                source[base - tap * dilation : base - tap * dilation + rows, :].astype(jnp.bfloat16)
                for tap in range(3)
            ]
            output = jnp.dot(
                jnp.concatenate(taps, axis=1), filters[layer], preferred_element_type=jnp.float32
            )
            mean = jnp.mean(output, axis=-1, keepdims=True)
            centred = output - mean
            spread = jnp.mean(centred * centred, axis=-1, keepdims=True)
            active = jnp.maximum(
                centred * lax.rsqrt(spread + epsilon) * gain_ref[layer : layer + 1, :], 0.0
            )
            if layer % 2 == 1:
                active = active + target[base : base + rows, :]
            active = active.astype(jnp.bfloat16)
            if layer == layers - 1:
                result[begin : begin + rows, :] = active
                copy = pltpu.make_async_copy(
                    result.at[pl.ds(begin, rows), :],
                    out_ref.at[pl.ds(begin, rows), :],
                    out_sems.at[len(out_copies)],
                )
                copy.start()
                out_copies.append(copy)
            else:
                target[base : base + rows, :] = active.astype(jnp.float32)
    for copy in out_copies:
        copy.wait()


def swapped(array, axis, distance):
    pairs = [(source, source ^ distance) for source in range(lax.axis_size(axis))]
    return lax.ppermute(array, axis, pairs)


def block_place(number, side):
    kind = number % 4
    bits = (2 if kind in (1, 3) else 0) + number // 4
    return bits, side if kind < 2 else 1 - side


def ordered_filters(blocks, me):
    count = blocks[0].shape[0]
    owners = 4 * count
    half = blocks[0].shape[1]
    layers = 2 * half
    whole = jnp.zeros((owners, layers) + blocks[0].shape[2:], blocks[0].dtype)
    for number, block in enumerate(blocks):
        bits, side = block_place(number, me[1])
        for shard in range(block.shape[0]):
            owner = me[0] ^ (4 * shard + bits)
            whole = lax.dynamic_update_slice(whole, block[shard][None], (owner, side * half, 0, 0))
    return whole.transpose(1, 0, 2, 3).reshape(layers, -1, whole.shape[-1])


def carried_rows(returning, home, entry, stores):
    copies = lax.axis_size("rep")
    me = lax.axis_index("rep")
    by_position = stores.transpose(1, 0, 2)
    positions, _, channels = by_position.shape
    carried = jnp.zeros((positions, channels), stores.dtype)
    for shift in range(copies):
        arrived = by_position
        if shift:
            pairs = [(source, (source + shift) % copies) for source in range(copies)]
            arrived = lax.ppermute(by_position, "rep", pairs)
        wanted = (returning[0] > 0) & (home[0] == (me + copies - shift) % copies)
        chosen = lax.dynamic_index_in_dim(arrived, entry[0], 1, keepdims=False)
        carried = jnp.where(wanted, chosen, carried)
    return carried.astype(jnp.float32)


def local(
    bag_rows, bag_owner, bag_weight, tables, returning, home, entry, stores, conv_weight, norm_gain
):
    owners = lax.axis_size("table")
    samples_here, slot_count, bag_width = bag_rows.shape
    token_count = samples_here * slot_count
    shard_rows = tables.shape[1]
    row_width = tables.shape[2]
    channels = conv_weight.shape[-1]
    capacity = min(token_count, (3 * token_count * bag_width + 2 * owners - 1) // (2 * owners))
    cuts = [0] + [round(capacity * end) // 16 * 16 for end in part_ends]
    early = cuts[-2]
    late = token_count - early
    smem = pl.BlockSpec(memory_space=pltpu.SMEM)
    vmem = pl.BlockSpec(memory_space=pltpu.VMEM)
    anywhere = pl.BlockSpec(memory_space=pl.ANY)

    me = jnp.stack([lax.axis_index("table"), lax.axis_index("rep") % 2]).astype(jnp.int32)
    half = conv_weight.shape[0] // 2
    shard = lax.dynamic_slice_in_dim(conv_weight, me[1] * half, half, 0)
    middle = owners // 8
    line = [shard] + [swapped(shard, "table", 4 * step) for step in range(1, middle + 1)]
    state = carried_rows(returning, home, entry, stores)
    rows_by_slot = bag_rows.reshape(token_count, bag_width).T
    owner_by_slot = bag_owner.reshape(token_count, bag_width).T
    requests, place = pl.pallas_call(
        functools.partial(prep_kernel, cuts, shard_rows),
        out_shape=(
            jax.ShapeDtypeStruct((owners, 1, capacity), jnp.int32),
            jax.ShapeDtypeStruct((bag_width, token_count), jnp.int32),
        ),
        in_specs=[vmem, vmem],
        out_specs=(vmem, vmem),
        compiler_params=pltpu.CompilerParams(vmem_limit_bytes=8 * megabyte),
        name="prep",
    )(rows_by_slot, owner_by_slot)
    received = lax.all_to_all(requests, "table", split_axis=0, concat_axis=0, tiled=True)
    received = received.reshape(owners * capacity)
    flat_table = tables.reshape(-1, row_width)
    returned = []
    sent = []
    for number in range(len(part_ends)):
        piece = cuts[number + 1] - cuts[number]
        if number == 1:
            middle_shard = tie(line[middle], received)
            forwarded = [swapped(middle_shard, "table", 4 * step) for step in range(1, middle)]
            line = line[:middle] + [middle_shard] + forwarded
        earlier = sent[-1:] if sent else line[1:]
        sent.append(
            pl.pallas_call(
                functools.partial(gather_kernel, capacity, cuts[number]),
                out_shape=jax.ShapeDtypeStruct((owners, piece, row_width), jnp.bfloat16),
                in_specs=[anywhere] * (2 + len(earlier)),
                out_specs=anywhere,
                scratch_shapes=[
                    pltpu.VMEM(flat_table.shape, jnp.bfloat16),
                    pltpu.VMEM(flat_table.shape, jnp.float32),
                    pltpu.VMEM((piece, row_width), jnp.float32),
                    pltpu.VMEM((owners, piece, row_width), jnp.bfloat16),
                    pltpu.SMEM((owners * capacity,), jnp.int32),
                    pltpu.SemaphoreType.DMA,
                    pltpu.SemaphoreType.DMA((8,)),
                    pltpu.SemaphoreType.DMA((owners,)),
                ],
                compiler_params=pltpu.CompilerParams(vmem_limit_bytes=58 * megabyte),
                cost_estimate=pl.CostEstimate(
                    flops=0, bytes_accessed=20 * megabyte, transcendentals=0
                ),
                name="owner_gather",
            )(received, flat_table, *earlier)
        )
    line = jnp.stack(line)
    by_table = swapped(line, "table", 2)
    by_rep = swapped(line, "rep", 1)
    by_table = tie(by_table, state)
    corner = swapped(by_table, "rep", 1)
    gates = [[], [sent[2]] + forwarded, [state, by_table, by_rep]]
    for rows, gate in zip(sent, gates):
        if returned:
            rows = tie(rows, returned[-1][: 16 if len(returned) > 1 else None], *gate)
        arrived = lax.all_to_all(rows, "table", split_axis=0, concat_axis=0, tiled=True)
        returned.append(arrived.reshape(-1, row_width))
    weight_by_slot = bag_weight.reshape(token_count, bag_width).T
    pooled = pl.pallas_call(
        pool_kernel,
        out_shape=jax.ShapeDtypeStruct((early, channels), jnp.bfloat16),
        in_specs=[smem] + [vmem] * len(returned),
        out_specs=vmem,
        scratch_shapes=[
            pltpu.VMEM((owners * early, row_width), jnp.float32),
            pltpu.VMEM((bag_width, early, row_width), jnp.float32),
        ],
        compiler_params=pltpu.CompilerParams(vmem_limit_bytes=32 * megabyte),
        cost_estimate=pl.CostEstimate(
            flops=0, bytes_accessed=24 * megabyte, transcendentals=0
        ),
        name="pool",
    )(place, weight_by_slot, *returned[:-1])
    corner = tie(corner, pooled)
    filters = [line, by_table, by_rep, corner]
    filters = filters + [swapped(block, "table", 1) for block in filters]
    if conv_weight.shape[1] % 16:
        filters = [ordered_filters(filters, me)]

    hidden = pl.pallas_call(
        functools.partial(stage_kernel, len(returned), len(filters)),
        out_shape=jax.ShapeDtypeStruct((token_count, channels), jnp.bfloat16),
        in_specs=[smem] * 2 + [vmem] * (4 + len(returned)) + [anywhere] * len(filters),
        out_specs=anywhere,
        scratch_shapes=[
            pltpu.VMEM((owners * cuts[-1], row_width), jnp.float32),
            pltpu.VMEM((bag_width, late, row_width), jnp.float32),
            pltpu.VMEM((conv_weight.shape[0], 3 * channels, channels), jnp.bfloat16),
            pltpu.VMEM((token_count + 16, channels), jnp.float32),
            pltpu.VMEM((token_count + 16, channels), jnp.float32),
            pltpu.VMEM((token_count, channels), jnp.bfloat16),
            pltpu.SemaphoreType.DMA((2 * owners,)),
            pltpu.SemaphoreType.DMA(((token_count + 255) // 256,)),
        ],
        compiler_params=pltpu.CompilerParams(vmem_limit_bytes=56 * megabyte),
        cost_estimate=pl.CostEstimate(
            flops=2 * token_count * 3 * channels * channels * conv_weight.shape[0],
            bytes_accessed=24 * megabyte,
            transcendentals=0,
        ),
        name="stage",
    )(place, me, weight_by_slot, state, norm_gain, pooled, *returned, *filters)
    return hidden.reshape(samples_here, slot_count, channels)


def solution(mesh):
    in_specs = (
        P(("table", "rep"), None, None),
        P(("table", "rep"), None, None),
        P(("table", "rep"), None, None),
        P(None, "table", None),
        P(("table", "rep")),
        P(("table", "rep")),
        P(("table", "rep")),
        P(("table", "rep"), None, None),
        P(None, "table", None),
        P(),
    )
    out_specs = P(("table", "rep"), None, None)
    return jax.shard_map(local, mesh=mesh, in_specs=in_specs, out_specs=out_specs, check_vma=False)
```

profile of v0, /device:TPU:0, one launch (start us, length us, event | category | flops | bytes accessed | tf_op | source)
XLA Modules:
  0.0 134.1 jit_solution(14507207361492650574)
XLA Ops:
  0.0 1.0 copy-done
  1.0 4.1 %collective-permute-start.2 = (bf16[2,96,512]{2,1,0:T(8,128)(2,1)S(1)}, bf16[2,96,512]{2,1,0:T(8,128)(2,1)S(1)}, u32[]{:S(2)}, u32[]{:S(2)}) collective-permute-start(bf16[2,96,512]{2,1,0:T(8,128)(2,1)S(1)} %constant_dynamic-slice_fusion), channel_id=1, source_target_pairs={{0,16},{2,18},{4,20},{6,22},{8,24},{10,26},{12,28},{14,30},{16,0},... | collective-permute-start | bytes 589832 | tf_op jit(solution)/shard_map/ppermute | solution.py:243
  5.1 1.6 %collective-permute-start.1 = (bf16[2,96,512]{2,1,0:T(8,128)(2,1)S(1)}, bf16[2,96,512]{2,1,0:T(8,128)(2,1)S(1)}, u32[]{:S(2)}, u32[]{:S(2)}) collective-permute-start(bf16[2,96,512]{2,1,0:T(8,128)(2,1)S(1)} %constant_dynamic-slice_fusion), channel_id=1, source_target_pairs={{0,8},{2,10},{4,12},{6,14},{8,0},{10,2},{12,4},{14,6},{16,24},{18,... | collective-permute-start | bytes 589832 | tf_op jit(solution)/shard_map/ppermute | solution.py:243
  6.7 0.8 copy-done.7
  7.5 0.8 copy-done.8
  8.2 1.2 prep.1
  9.5 10.0 %all_to_all.20 = s32[16,1,768]{2,1,0:T(1,128)} all-to-all(s32[16,1,768]{2,1,0:T(1,128)S(1)} %get-tuple-element.8), channel_id=1, replica_groups=mesh['table'=16,'rep'=2] {'table'}, dimensions={0} | all-to-all | bytes 98304 | tf_op jit(solution)/shard_map/all_to_all | solution.py:319
  19.5 0.0 collective-permute-done.2.refs_1_.refs_0_
  19.5 0.0 collective-permute-done.1.refs_0_
  19.5 0.7 copy-done.10
  20.2 0.1 copy-done.14
  20.3 5.4 %owner_gather.3.refs_0_ = bf16[16,192,128]{2,1,0:T(8,128)(2,1)} custom-call(s32[12288]{0:T(1024)} %bitcast.53, bf16[8192,128]{1,0:T(8,128)(2,1)} %bitcast.49, bf16[2,96,512]{2,1,0:T(8,128)(2,1)} %copy-done.14, bf16[2,96,512]{2,1,0:T(8,128)(2,1)} %copy-done.10), custom_call_target="tpu_custom_call" | custom-call | bytes 20971520 | tf_op jit(solution)/shard_map/owner_gather/pallas_call | solution.py:332
  25.6 3.6 %all-to-all-start.1 = ((bf16[16,192,128]{2,1,0:T(8,128)(2,1)}), bf16[16,192,128]{2,1,0:T(8,128)(2,1)S(1)}, u32[]{:S(2)}, u32[]{:S(2)}) async-start(bf16[16,192,128]{2,1,0:T(8,128)(2,1)} %owner_gather.3.refs_0_), calls=%async_computation.1 | async-start | bytes 1572864 | tf_op jit(solution)/shard_map/all_to_all | solution.py:363
  29.3 1.9 %collective-permute-start.3 = (bf16[2,96,512]{2,1,0:T(8,128)(2,1)}, bf16[2,96,512]{2,1,0:T(8,128)(2,1)S(1)}, u32[]{:S(2)}, u32[]{:S(2)}) collective-permute-start(bf16[2,96,512]{2,1,0:T(8,128)(2,1)} %tie.5), channel_id=1, source_target_pairs={{0,8},{2,10},{4,12},{6,14},{8,0},{10,2},{12,4},{14,6},{16,24},{18,... | collective-permute-start | bytes 589832 | tf_op jit(solution)/shard_map/ppermute | solution.py:243
  31.2 9.3 %owner_gather.4.refs_0_ = bf16[16,448,128]{2,1,0:T(8,128)(2,1)} custom-call(s32[12288]{0:T(1024)} %bitcast.55, bf16[8192,128]{1,0:T(8,128)(2,1)} %bitcast.50, bf16[16,192,128]{2,1,0:T(8,128)(2,1)} %owner_gather.3.refs_0_), custom_call_target="tpu_custom_call" | custom-call | bytes 20971520 | tf_op jit(solution)/shard_map/owner_gather/pallas_call | solution.py:332
  40.5 4.4 %owner_gather.5.refs_2_.refs_0_ = bf16[16,128,128]{2,1,0:T(8,128)(2,1)} custom-call(s32[12288]{0:T(1024)} %bitcast.56, bf16[8192,128]{1,0:T(8,128)(2,1)} %bitcast.51, bf16[16,448,128]{2,1,0:T(8,128)(2,1)} %owner_gather.4.refs_0_), custom_call_target="tpu_custom_call" | custom-call | bytes 20971520 | tf_op jit(solution)/shard_map/owner_gather/pallas_call | solution.py:332
  44.9 4.3 %collective-permute-done.3.refs_3_ = bf16[2,96,512]{2,1,0:T(8,128)(2,1)S(1)} collective-permute-done((bf16[2,96,512]{2,1,0:T(8,128)(2,1)}, bf16[2,96,512]{2,1,0:T(8,128)(2,1)S(1)}, u32[]{:S(2)}, u32[]{:S(2)}) %collective-permute-start.3) | collective-permute-done | bytes 196640 | tf_op jit(solution)/shard_map/ppermute | solution.py:243
  49.2 0.0 all-to-all-done.1
  49.2 0.7 copy-done.12
  49.9 0.3 copy-done.2
  50.2 5.0 %all-to-all-start.2 = ((bf16[16,448,128]{2,1,0:T(8,128)(2,1)}), bf16[16,448,128]{2,1,0:T(8,128)(2,1)S(1)}, u32[]{:S(2)}, u32[]{:S(2)}) async-start(bf16[16,448,128]{2,1,0:T(8,128)(2,1)} %tie.6), calls=%async_computation.2 | async-start | bytes 3670016 | tf_op jit(solution)/shard_map/all_to_all | solution.py:363
  55.1 0.0 copy-start.16
  55.2 1.0 pad_maximum_fusion.refs_3_
  56.2 1.9 %collective-permute-start.4 = (bf16[4,2,96,512]{3,2,1,0:T(8,128)(2,1)}, bf16[4,2,96,512]{3,2,1,0:T(8,128)(2,1)S(1)}, u32[]{:S(2)}, u32[]{:S(2)}) collective-permute-start(bf16[4,2,96,512]{3,2,1,0:T(8,128)(2,1)} %pad_maximum_fusion.refs_3_), channel_id=1, source_target_pairs={{0,4},{2,6},{4,0},{6,2},{8,12},{10,14},{12,8},{14,10},{16,20},{18,... | collective-permute-start | bytes 2359304 | tf_op jit(solution)/shard_map/ppermute | solution.py:243
  58.1 0.1 copy.21
  58.2 1.6 %collective-permute-start = (bf16[30,8,512]{2,0,1:T(8,128)(2,1)S(1)}, bf16[30,8,512]{2,0,1:T(8,128)(2,1)}, u32[]{:S(2)}, u32[]{:S(2)}) collective-permute-start(bf16[30,8,512]{2,0,1:T(8,128)(2,1)S(1)} %bitcast.59), channel_id=1, source_target_pairs={{0,1},{1,0},{2,3},{3,2},{4,5},{5,4},{6,7},{7,6},{8,9},{9,8},{10,11... | collective-permute-start | bytes 737288 | tf_op jit(solution)/shard_map/ppermute | solution.py:276
  59.7 0.5 collective-permute-start.5
  62.2 5.3 %collective-permute-done = bf16[30,8,512]{2,0,1:T(8,128)(2,1)} collective-permute-done((bf16[30,8,512]{2,0,1:T(8,128)(2,1)S(1)}, bf16[30,8,512]{2,0,1:T(8,128)(2,1)}, u32[]{:S(2)}, u32[]{:S(2)}) %collective-permute-start) | collective-permute-done | bytes 245792 | tf_op jit(solution)/shard_map/ppermute | solution.py:276
  67.5 1.4 %fusion.refs_1_.refs_2_.carried_ref = f32[30,512]{1,0:T(8,128)} fusion(bf16[8,30,512]{2,1,0:T(8,128)(2,1)S(1)} %copy.21, s32[]{:T(128)S(6)} %select_n.43, bf16[30,8,512]{2,0,1:T(8,128)(2,1)} %collective-permute-done, pred[]{:T(512)S(6)} %and.25, pred[]{:T(512)S(6)} %and.23), kind=kLoop, calls=%fused_computation.2 | loop fusion | flops 46080 | bytes 122886 | tf_op jit(solution)/shard_map/convert_element_type | solution.py:280
  68.9 25.8 %collective-permute-done.4.refs_0_ = bf16[4,2,96,512]{3,2,1,0:T(8,128)(2,1)S(1)} collective-permute-done((bf16[4,2,96,512]{3,2,1,0:T(8,128)(2,1)}, bf16[4,2,96,512]{3,2,1,0:T(8,128)(2,1)S(1)}, u32[]{:S(2)}, u32[]{:S(2)}) %collective-permute-start.4) | collective-permute-done | bytes 786464 | tf_op jit(solution)/shard_map/ppermute | solution.py:243
  94.8 1.0 copy-done.9
  95.7 1.5 %collective-permute-start.6 = (bf16[4,2,96,512]{3,2,1,0:T(8,128)(2,1)}, bf16[4,2,96,512]{3,2,1,0:T(8,128)(2,1)}, u32[]{:S(2)}, u32[]{:S(2)}) collective-permute-start(bf16[4,2,96,512]{3,2,1,0:T(8,128)(2,1)} %tie.7.refs_3_.refs_4_), channel_id=1, source_target_pairs={{0,1},{1,0},{2,3},{3,2},{4,5},{5,4},{6,7},{7,6},{8,9},{9,8},{10,11... | collective-permute-start | bytes 2359304 | tf_op jit(solution)/shard_map/ppermute | solution.py:243
  97.2 0.6 slice.4.refs_1_
  97.9 0.0 collective-permute-done.5.refs_4_.refs_5_
  97.9 4.9 %all-to-all-start.3 = ((bf16[16,128,128]{2,1,0:T(8,128)(2,1)}), bf16[16,128,128]{2,1,0:T(8,128)(2,1)}, u32[]{:S(2)}, u32[]{:S(2)}) async-start(bf16[16,128,128]{2,1,0:T(8,128)(2,1)} %tie.8), calls=%async_computation.3 | async-start | bytes 1048576 | tf_op jit(solution)/shard_map/all_to_all | solution.py:363
  102.8 0.4 collective-permute-start.7
  103.2 0.2 collective-permute-start.8
  103.4 0.3 collective-permute-start.9
  103.7 9.1 %pool.1.refs_1_.pooled_ref = bf16[640,512]{1,0:T(8,128)(2,1)S(1)} custom-call(s32[8,1024]{1,0:T(8,128)S(1)} %get-tuple-element.7.place_ref, f32[8,1024]{1,0:T(8,128)S(1)} %bitcast.46, bf16[3072,128]{1,0:T(8,128)(2,1)S(1)} %bitcast.44, bf16[7168,128]{1,0:T(8,128)(2,1)S(1)} %bitcast.40), custom_call_target="tpu_custom_call" | custom-call | bytes 25165824 | tf_op jit(solution)/shard_map/pool/pallas_call | solution.py:366
  112.8 0.8 copy-done.4
  113.7 1.5 %collective-permute-done.6.refs_0_ = bf16[4,2,96,512]{3,2,1,0:T(8,128)(2,1)} collective-permute-done((bf16[4,2,96,512]{3,2,1,0:T(8,128)(2,1)}, bf16[4,2,96,512]{3,2,1,0:T(8,128)(2,1)}, u32[]{:S(2)}, u32[]{:S(2)}) %collective-permute-start.6) | collective-permute-done | bytes 786464 | tf_op jit(solution)/shard_map/ppermute | solution.py:243
  115.2 0.6 pad_add_fusion.me_ref
  115.8 0.0 collective-permute-done.7.refs_7_
  115.8 0.0 collective-permute-done.9.refs_9_
  115.8 0.0 collective-permute-done.8.refs_8_
  115.8 1.9 %collective-permute-done.10.refs_10_ = bf16[4,2,96,512]{3,2,1,0:T(8,128)(2,1)S(1)} collective-permute-done((bf16[4,2,96,512]{3,2,1,0:T(8,128)(2,1)}, bf16[4,2,96,512]{3,2,1,0:T(8,128)(2,1)S(1)}, u32[]{:S(2)}, u32[]{:S(2)}) %collective-permute-start.10) | collective-permute-done | bytes 786464 | tf_op jit(solution)/shard_map/ppermute | solution.py:243
  117.7 0.9 copy-done.17
  118.5 15.5 %stage.1 = bf16[1024,512]{1,0:T(8,128)(2,1)} custom-call(s32[8,1024]{1,0:T(8,128)} %copy-done.6, s32[2]{0:T(128)} %pad_add_fusion.me_ref, f32[8,1024]{1,0:T(8,128)} %bitcast.45, f32[30,512]{1,0:T(8,128)} %fusion.refs_1_.refs_2_.carried_ref, f32[4,512]{1,0:T(4,128)} %gain_ref.1, bf16[640,512]{1,0:T(8,128)(2,1)} %copy-done.4, bf16[3072,128]{1,0:T(8,128)(2,1)} %bitcast.43, ...), custom_call_target="tpu_custom_call" | custom-call | flops 6442450944 | bytes 25165824 | tf_op jit(solution)/shard_map/stage/pallas_call | solution.py:387
  (35 shorter events, 0.1 us)
Async XLA Ops:
  0.0 1.0 copy-start
  1.0 18.5 %collective-permute-start.2 = (bf16[2,96,512]{2,1,0:T(8,128)(2,1)S(1)}, bf16[2,96,512]{2,1,0:T(8,128)(2,1)S(1)}, u32[]{:S(2)}, u32[]{:S(2)}) collective-permute-start(bf16[2,96,512]{2,1,0:T(8,128)(2,1)S(1)} %constant_dynamic-slice_fusion), channel_id=1, source_target_pairs={{0,16},{2,18},{4,20},{6,22},{8,24},{10,26},{12,28},{14,30},{16,0},... | collective-permute-start | bytes 589832 | tf_op jit(solution)/shard_map/ppermute | solution.py:243
  5.1 14.4 %collective-permute-start.1 = (bf16[2,96,512]{2,1,0:T(8,128)(2,1)S(1)}, bf16[2,96,512]{2,1,0:T(8,128)(2,1)S(1)}, u32[]{:S(2)}, u32[]{:S(2)}) collective-permute-start(bf16[2,96,512]{2,1,0:T(8,128)(2,1)S(1)} %constant_dynamic-slice_fusion), channel_id=1, source_target_pairs={{0,8},{2,10},{4,12},{6,14},{8,0},{10,2},{12,4},{14,6},{16,24},{18,... | collective-permute-start | bytes 589832 | tf_op jit(solution)/shard_map/ppermute | solution.py:243
  6.7 0.8 copy-start.7
  7.5 0.8 copy-start.8
  9.5 94.3 %copy-start.6 = (s32[8,1024]{1,0:T(8,128)}, s32[8,1024]{1,0:T(8,128)S(1)}, u32[]{:S(2)}) copy-start(s32[8,1024]{1,0:T(8,128)S(1)} %get-tuple-element.7.place_ref) | copy-start | bytes 98308
  19.5 0.7 copy-start.10
  19.5 0.7 copy-start.14
  25.6 23.5 %all-to-all-start.1 = ((bf16[16,192,128]{2,1,0:T(8,128)(2,1)}), bf16[16,192,128]{2,1,0:T(8,128)(2,1)S(1)}, u32[]{:S(2)}, u32[]{:S(2)}) async-start(bf16[16,192,128]{2,1,0:T(8,128)(2,1)} %owner_gather.3.refs_0_), calls=%async_computation.1 | async-start | bytes 1572864 | tf_op jit(solution)/shard_map/all_to_all | solution.py:363
  29.3 19.9 %collective-permute-start.3 = (bf16[2,96,512]{2,1,0:T(8,128)(2,1)}, bf16[2,96,512]{2,1,0:T(8,128)(2,1)S(1)}, u32[]{:S(2)}, u32[]{:S(2)}) collective-permute-start(bf16[2,96,512]{2,1,0:T(8,128)(2,1)} %tie.5), channel_id=1, source_target_pairs={{0,8},{2,10},{4,12},{6,14},{8,0},{10,2},{12,4},{14,6},{16,24},{18,... | collective-permute-start | bytes 589832 | tf_op jit(solution)/shard_map/ppermute | solution.py:243
  49.2 0.7 copy-start.12
  49.2 1.0 copy-start.2
  50.1 5.0 %copy-start.11 = (bf16[2,96,512]{2,1,0:T(8,128)(2,1)S(1)}, bf16[2,96,512]{2,1,0:T(8,128)(2,1)}, u32[]{:S(2)}) copy-start(bf16[2,96,512]{2,1,0:T(8,128)(2,1)} %tie.5) | copy-start | bytes 589828
  50.1 5.0 %copy-start.13 = (bf16[2,96,512]{2,1,0:T(8,128)(2,1)S(1)}, bf16[2,96,512]{2,1,0:T(8,128)(2,1)}, u32[]{:S(2)}) copy-start(bf16[2,96,512]{2,1,0:T(8,128)(2,1)} %copy-done.12) | copy-start | bytes 589828
  50.2 5.0 %copy-start.15 = (bf16[2,96,512]{2,1,0:T(8,128)(2,1)S(1)}, bf16[2,96,512]{2,1,0:T(8,128)(2,1)}, u32[]{:S(2)}) copy-start(bf16[2,96,512]{2,1,0:T(8,128)(2,1)} %copy-done.14) | copy-start | bytes 589828
  50.2 47.1 %all-to-all-start.2 = ((bf16[16,448,128]{2,1,0:T(8,128)(2,1)}), bf16[16,448,128]{2,1,0:T(8,128)(2,1)S(1)}, u32[]{:S(2)}, u32[]{:S(2)}) async-start(bf16[16,448,128]{2,1,0:T(8,128)(2,1)} %tie.6), calls=%async_computation.2 | async-start | bytes 3670016 | tf_op jit(solution)/shard_map/all_to_all | solution.py:363
  55.1 3.0 %copy-start.16 = (bf16[8,30,512]{2,0,1:T(8,128)(2,1)S(1)}, bf16[8,30,512]{2,0,1:T(8,128)(2,1)}, u32[]{:S(2)}) copy-start(bf16[8,30,512]{2,0,1:T(8,128)(2,1)} %param.17) | copy-start | bytes 737284
  56.2 38.6 %collective-permute-start.4 = (bf16[4,2,96,512]{3,2,1,0:T(8,128)(2,1)}, bf16[4,2,96,512]{3,2,1,0:T(8,128)(2,1)S(1)}, u32[]{:S(2)}, u32[]{:S(2)}) collective-permute-start(bf16[4,2,96,512]{3,2,1,0:T(8,128)(2,1)} %pad_maximum_fusion.refs_3_), channel_id=1, source_target_pairs={{0,4},{2,6},{4,0},{6,2},{8,12},{10,14},{12,8},{14,10},{16,20},{18,... | collective-permute-start | bytes 2359304 | tf_op jit(solution)/shard_map/ppermute | solution.py:243
  58.2 9.4 %collective-permute-start = (bf16[30,8,512]{2,0,1:T(8,128)(2,1)S(1)}, bf16[30,8,512]{2,0,1:T(8,128)(2,1)}, u32[]{:S(2)}, u32[]{:S(2)}) collective-permute-start(bf16[30,8,512]{2,0,1:T(8,128)(2,1)S(1)} %bitcast.59), channel_id=1, source_target_pairs={{0,1},{1,0},{2,3},{3,2},{4,5},{5,4},{6,7},{7,6},{8,9},{9,8},{10,11... | collective-permute-start | bytes 737288 | tf_op jit(solution)/shard_map/ppermute | solution.py:276
  59.7 38.1 %collective-permute-start.5 = (bf16[4,2,96,512]{3,2,1,0:T(8,128)(2,1)}, bf16[4,2,96,512]{3,2,1,0:T(8,128)(2,1)}, u32[]{:S(2)}, u32[]{:S(2)}) collective-permute-start(bf16[4,2,96,512]{3,2,1,0:T(8,128)(2,1)} %pad_maximum_fusion.refs_3_), channel_id=1, source_target_pairs={{0,1},{1,0},{2,3},{3,2},{4,5},{5,4},{6,7},{7,6},{8,9},{9,8},{10,11... | collective-permute-start | bytes 2359304 | tf_op jit(solution)/shard_map/ppermute | solution.py:243
  94.8 1.0 copy-start.9
  95.7 19.4 %collective-permute-start.6 = (bf16[4,2,96,512]{3,2,1,0:T(8,128)(2,1)}, bf16[4,2,96,512]{3,2,1,0:T(8,128)(2,1)}, u32[]{:S(2)}, u32[]{:S(2)}) collective-permute-start(bf16[4,2,96,512]{3,2,1,0:T(8,128)(2,1)} %tie.7.refs_3_.refs_4_), channel_id=1, source_target_pairs={{0,1},{1,0},{2,3},{3,2},{4,5},{5,4},{6,7},{7,6},{8,9},{9,8},{10,11... | collective-permute-start | bytes 2359304 | tf_op jit(solution)/shard_map/ppermute | solution.py:243
  97.2 6.5 %copy-start.1 = (bf16[16,448,128]{2,1,0:T(8,128)(2,1)}, bf16[16,448,128]{2,1,0:T(8,128)(2,1)S(1)}, u32[]{:S(2)}) copy-start(bf16[16,448,128]{2,1,0:T(8,128)(2,1)S(1)} %all-to-all-done.2) | copy-start | bytes 5505028
  97.9 5.9 %copy-start.3 = (bf16[16,192,128]{2,1,0:T(8,128)(2,1)S(1)}, bf16[16,192,128]{2,1,0:T(8,128)(2,1)}, u32[]{:S(2)}) copy-start(bf16[16,192,128]{2,1,0:T(8,128)(2,1)} %copy-done.2) | copy-start | bytes 2359300
  97.9 5.9 %copy-start.5 = (f32[1,1024,8]{1,2,0:T(8,128)S(1)}, f32[1,1024,8]{1,2,0:T(8,128)}, u32[]{:S(2)}) copy-start(f32[1,1024,8]{1,2,0:T(8,128)} %param.12) | copy-start | bytes 98308
  97.9 19.8 %all-to-all-start.3 = ((bf16[16,128,128]{2,1,0:T(8,128)(2,1)}), bf16[16,128,128]{2,1,0:T(8,128)(2,1)}, u32[]{:S(2)}, u32[]{:S(2)}) async-start(bf16[16,128,128]{2,1,0:T(8,128)(2,1)} %tie.8), calls=%async_computation.3 | async-start | bytes 1048576 | tf_op jit(solution)/shard_map/all_to_all | solution.py:363
  102.8 12.9 %collective-permute-start.7 = (bf16[4,2,96,512]{3,2,1,0:T(8,128)(2,1)}, bf16[4,2,96,512]{3,2,1,0:T(8,128)(2,1)}, u32[]{:S(2)}, u32[]{:S(2)}) collective-permute-start(bf16[4,2,96,512]{3,2,1,0:T(8,128)(2,1)} %pad_maximum_fusion.refs_3_), channel_id=1, source_target_pairs={{0,2},{2,0},{4,6},{6,4},{8,10},{10,8},{12,14},{14,12},{16,18},{18,... | collective-permute-start | bytes 2359304 | tf_op jit(solution)/shard_map/ppermute | solution.py:243
  103.2 12.5 %collective-permute-start.8 = (bf16[4,2,96,512]{3,2,1,0:T(8,128)(2,1)}, bf16[4,2,96,512]{3,2,1,0:T(8,128)(2,1)}, u32[]{:S(2)}, u32[]{:S(2)}) collective-permute-start(bf16[4,2,96,512]{3,2,1,0:T(8,128)(2,1)} %tie.7.refs_3_.refs_4_), channel_id=1, source_target_pairs={{0,2},{2,0},{4,6},{6,4},{8,10},{10,8},{12,14},{14,12},{16,18},{18,... | collective-permute-start | bytes 2359304 | tf_op jit(solution)/shard_map/ppermute | solution.py:243
  103.4 12.4 %collective-permute-start.9 = (bf16[4,2,96,512]{3,2,1,0:T(8,128)(2,1)}, bf16[4,2,96,512]{3,2,1,0:T(8,128)(2,1)}, u32[]{:S(2)}, u32[]{:S(2)}) collective-permute-start(bf16[4,2,96,512]{3,2,1,0:T(8,128)(2,1)} %collective-permute-done.5.refs_4_.refs_5_), channel_id=1, source_target_pairs={{0,2},{2,0},{4,6},{6,4},{8,10},{10,8},{12,14},{14,12},{16,18},{18,... | collective-permute-start | bytes 2359304 | tf_op jit(solution)/shard_map/ppermute | solution.py:243
  112.8 0.8 copy-start.4
  115.2 2.5 %collective-permute-start.10 = (bf16[4,2,96,512]{3,2,1,0:T(8,128)(2,1)}, bf16[4,2,96,512]{3,2,1,0:T(8,128)(2,1)S(1)}, u32[]{:S(2)}, u32[]{:S(2)}) collective-permute-start(bf16[4,2,96,512]{3,2,1,0:T(8,128)(2,1)} %tie.9.refs_6_), channel_id=1, source_target_pairs={{0,2},{2,0},{4,6},{6,4},{8,10},{10,8},{12,14},{14,12},{16,18},{18,... | collective-permute-start | bytes 2359304 | tf_op jit(solution)/shard_map/ppermute | solution.py:243
  117.6 0.9 copy-start.17
where the time goes:
time: 135 us; the launch traced here: 134 us
  Pallas kernels  44.8 us (33%)
  waiting for transfers between devices  38.8 us (29%)
  starting transfers between devices  27.5 us (20%)
  blocking collectives  10 us (7%)
  local copies, waits for them, and re-layouts  7.67 us (6%)
  other arithmetic  2.96 us (2%)
  between operations  2.31 us (2%)
    ppermute x10, waiting for transfers between devices, swapped(): return lax.ppermute(array, axis, pairs)  33.5 us
    pallas_call x3, Pallas kernels, local(): pl.pallas_call(functools.partial(gather_kernel, capacity, cuts[number]),...  19.1 us
    pallas_call x1, Pallas kernels, local(): pl.pallas_call(functools.partial(stage_kernel, len(returned), len(filters...  15.5 us
    all_to_all x3, starting transfers between devices, local(): lax.all_to_all(rows, 'table', split_axis=0, concat_axis=0, tiled=True)  13.5 us
    ppermute x10, starting transfers between devices, swapped(): return lax.ppermute(array, axis, pairs)  12.4 us
    all_to_all x1, blocking collectives, local(): lax.all_to_all(requests, 'table', split_axis=0, concat_axis=0, tiled=True)  10 us
    pallas_call x1, Pallas kernels, local(): pl.pallas_call(pool_kernel, out_shape=jax.ShapeDtypeStruct((early, channe...  9.05 us
    unnamed x37, local copies, waits for them, and re-layouts  7.02 us
  transfers between devices with their start and end apart: 14, of which 5 were waited for; matrix products, arithmetic and copies ran while one was open for 3% of the time, Pallas kernels for 18%

commit v1 on v0

--- a/solution.py
+++ b/solution.py
@@ -204,8 +204,8 @@
         source, target = (first_buf, second_buf) if layer % 2 == 0 else (second_buf, first_buf)
         source[front - span : front, :] = carried_ref[offset : offset + span, :]
         offset += span
-        for begin in range(0, slots, 256):
-            rows = min(256, slots - begin)
+        for begin in range(0, slots, 512):
+            rows = min(512, slots - begin)
             base = front + begin
             taps = [
                 source[base - tap * dilation : base - tap * dilation + rows, :].astype(jnp.bfloat16)

time: 135 us -> 135 us (level)
  no operation moved by 1% of the time
where the time goes in v1:
time: 135 us; the launch traced here: 134 us
  Pallas kernels  45.1 us (33%)
  waiting for transfers between devices  38.8 us (29%)
  starting transfers between devices  27.5 us (20%)
  blocking collectives  10 us (7%)
  local copies, waits for them, and re-layouts  7.67 us (6%)
  other arithmetic  2.96 us (2%)
  between operations  2.31 us (2%)
    ppermute x10, waiting for transfers between devices, swapped(): return lax.ppermute(array, axis, pairs)  33.5 us
    pallas_call x3, Pallas kernels, local(): pl.pallas_call(functools.partial(gather_kernel, capacity, cuts[number]),...  19.1 us
    pallas_call x1, Pallas kernels, local(): pl.pallas_call(functools.partial(stage_kernel, len(returned), len(filters...  15.7 us
    all_to_all x3, starting transfers between devices, local(): lax.all_to_all(rows, 'table', split_axis=0, concat_axis=0, tiled=True)  13.5 us
    ppermute x10, starting transfers between devices, swapped(): return lax.ppermute(array, axis, pairs)  12.4 us
    all_to_all x1, blocking collectives, local(): lax.all_to_all(requests, 'table', split_axis=0, concat_axis=0, tiled=True)  10 us
    pallas_call x1, Pallas kernels, local(): pl.pallas_call(pool_kernel, out_shape=jax.ShapeDtypeStruct((early, channe...  9.05 us
    unnamed x37, local copies, waits for them, and re-layouts  7.02 us
  transfers between devices with their start and end apart: 14, of which 5 were waited for; matrix products, arithmetic and copies ran while one was open for 3% of the time, Pallas kernels for 18%

profile of v1, /device:TPU:0, one launch (start us, length us, event | category | flops | bytes accessed | tf_op | source)
XLA Modules:
  0.0 134.4 jit_solution(4192226332319403048)
XLA Ops:
  0.0 1.0 copy-done
  1.0 4.1 %collective-permute-start.2 = (bf16[2,96,512]{2,1,0:T(8,128)(2,1)S(1)}, bf16[2,96,512]{2,1,0:T(8,128)(2,1)S(1)}, u32[]{:S(2)}, u32[]{:S(2)}) collective-permute-start(bf16[2,96,512]{2,1,0:T(8,128)(2,1)S(1)} %constant_dynamic-slice_fusion), channel_id=1, source_target_pairs={{0,16},{2,18},{4,20},{6,22},{8,24},{10,26},{12,28},{14,30},{16,0},... | collective-permute-start | bytes 589832 | tf_op jit(solution)/shard_map/ppermute | solution.py:243
  5.1 1.6 %collective-permute-start.1 = (bf16[2,96,512]{2,1,0:T(8,128)(2,1)S(1)}, bf16[2,96,512]{2,1,0:T(8,128)(2,1)S(1)}, u32[]{:S(2)}, u32[]{:S(2)}) collective-permute-start(bf16[2,96,512]{2,1,0:T(8,128)(2,1)S(1)} %constant_dynamic-slice_fusion), channel_id=1, source_target_pairs={{0,8},{2,10},{4,12},{6,14},{8,0},{10,2},{12,4},{14,6},{16,24},{18,... | collective-permute-start | bytes 589832 | tf_op jit(solution)/shard_map/ppermute | solution.py:243
  6.7 0.8 copy-done.7
  7.5 0.8 copy-done.8
  8.2 1.2 prep.1
  9.5 10.0 %all_to_all.20 = s32[16,1,768]{2,1,0:T(1,128)} all-to-all(s32[16,1,768]{2,1,0:T(1,128)S(1)} %get-tuple-element.8), channel_id=1, replica_groups=mesh['table'=16,'rep'=2] {'table'}, dimensions={0} | all-to-all | bytes 98304 | tf_op jit(solution)/shard_map/all_to_all | solution.py:319
  19.5 0.0 collective-permute-done.2.refs_1_.refs_0_
  19.5 0.7 copy-done.10
  20.2 0.1 copy-done.14
  20.3 5.4 %owner_gather.3.refs_0_ = bf16[16,192,128]{2,1,0:T(8,128)(2,1)} custom-call(s32[12288]{0:T(1024)} %bitcast.53, bf16[8192,128]{1,0:T(8,128)(2,1)} %bitcast.49, bf16[2,96,512]{2,1,0:T(8,128)(2,1)} %copy-done.14, bf16[2,96,512]{2,1,0:T(8,128)(2,1)} %copy-done.10), custom_call_target="tpu_custom_call" | custom-call | bytes 20971520 | tf_op jit(solution)/shard_map/owner_gather/pallas_call | solution.py:332
  25.6 3.6 %all-to-all-start.1 = ((bf16[16,192,128]{2,1,0:T(8,128)(2,1)}), bf16[16,192,128]{2,1,0:T(8,128)(2,1)S(1)}, u32[]{:S(2)}, u32[]{:S(2)}) async-start(bf16[16,192,128]{2,1,0:T(8,128)(2,1)} %owner_gather.3.refs_0_), calls=%async_computation.1 | async-start | bytes 1572864 | tf_op jit(solution)/shard_map/all_to_all | solution.py:363
  29.3 1.9 %collective-permute-start.3 = (bf16[2,96,512]{2,1,0:T(8,128)(2,1)}, bf16[2,96,512]{2,1,0:T(8,128)(2,1)S(1)}, u32[]{:S(2)}, u32[]{:S(2)}) collective-permute-start(bf16[2,96,512]{2,1,0:T(8,128)(2,1)} %tie.5), channel_id=1, source_target_pairs={{0,8},{2,10},{4,12},{6,14},{8,0},{10,2},{12,4},{14,6},{16,24},{18,... | collective-permute-start | bytes 589832 | tf_op jit(solution)/shard_map/ppermute | solution.py:243
  31.2 9.3 %owner_gather.4.refs_0_ = bf16[16,448,128]{2,1,0:T(8,128)(2,1)} custom-call(s32[12288]{0:T(1024)} %bitcast.55, bf16[8192,128]{1,0:T(8,128)(2,1)} %bitcast.50, bf16[16,192,128]{2,1,0:T(8,128)(2,1)} %owner_gather.3.refs_0_), custom_call_target="tpu_custom_call" | custom-call | bytes 20971520 | tf_op jit(solution)/shard_map/owner_gather/pallas_call | solution.py:332
  40.5 4.4 %owner_gather.5.refs_2_.refs_0_ = bf16[16,128,128]{2,1,0:T(8,128)(2,1)} custom-call(s32[12288]{0:T(1024)} %bitcast.56, bf16[8192,128]{1,0:T(8,128)(2,1)} %bitcast.51, bf16[16,448,128]{2,1,0:T(8,128)(2,1)} %owner_gather.4.refs_0_), custom_call_target="tpu_custom_call" | custom-call | bytes 20971520 | tf_op jit(solution)/shard_map/owner_gather/pallas_call | solution.py:332
  44.9 4.3 %collective-permute-done.3.refs_3_ = bf16[2,96,512]{2,1,0:T(8,128)(2,1)S(1)} collective-permute-done((bf16[2,96,512]{2,1,0:T(8,128)(2,1)}, bf16[2,96,512]{2,1,0:T(8,128)(2,1)S(1)}, u32[]{:S(2)}, u32[]{:S(2)}) %collective-permute-start.3) | collective-permute-done | bytes 196640 | tf_op jit(solution)/shard_map/ppermute | solution.py:243
  49.2 0.0 all-to-all-done.1
  49.2 0.7 copy-done.12
  49.9 0.3 copy-done.2
  50.2 5.0 %all-to-all-start.2 = ((bf16[16,448,128]{2,1,0:T(8,128)(2,1)}), bf16[16,448,128]{2,1,0:T(8,128)(2,1)S(1)}, u32[]{:S(2)}, u32[]{:S(2)}) async-start(bf16[16,448,128]{2,1,0:T(8,128)(2,1)} %tie.6), calls=%async_computation.2 | async-start | bytes 3670016 | tf_op jit(solution)/shard_map/all_to_all | solution.py:363
  55.1 0.0 copy-start.16
  55.2 1.0 pad_maximum_fusion.refs_3_
  56.2 1.9 %collective-permute-start.4 = (bf16[4,2,96,512]{3,2,1,0:T(8,128)(2,1)}, bf16[4,2,96,512]{3,2,1,0:T(8,128)(2,1)S(1)}, u32[]{:S(2)}, u32[]{:S(2)}) collective-permute-start(bf16[4,2,96,512]{3,2,1,0:T(8,128)(2,1)} %pad_maximum_fusion.refs_3_), channel_id=1, source_target_pairs={{0,4},{2,6},{4,0},{6,2},{8,12},{10,14},{12,8},{14,10},{16,20},{18,... | collective-permute-start | bytes 2359304 | tf_op jit(solution)/shard_map/ppermute | solution.py:243
  58.1 0.1 copy.21
  58.2 1.6 %collective-permute-start = (bf16[30,8,512]{2,0,1:T(8,128)(2,1)S(1)}, bf16[30,8,512]{2,0,1:T(8,128)(2,1)}, u32[]{:S(2)}, u32[]{:S(2)}) collective-permute-start(bf16[30,8,512]{2,0,1:T(8,128)(2,1)S(1)} %bitcast.59), channel_id=1, source_target_pairs={{0,1},{1,0},{2,3},{3,2},{4,5},{5,4},{6,7},{7,6},{8,9},{9,8},{10,11... | collective-permute-start | bytes 737288 | tf_op jit(solution)/shard_map/ppermute | solution.py:276
  59.7 0.5 collective-permute-start.5
  62.2 5.3 %collective-permute-done = bf16[30,8,512]{2,0,1:T(8,128)(2,1)} collective-permute-done((bf16[30,8,512]{2,0,1:T(8,128)(2,1)S(1)}, bf16[30,8,512]{2,0,1:T(8,128)(2,1)}, u32[]{:S(2)}, u32[]{:S(2)}) %collective-permute-start) | collective-permute-done | bytes 245792 | tf_op jit(solution)/shard_map/ppermute | solution.py:276
  67.5 1.4 %fusion.refs_1_.refs_2_.carried_ref = f32[30,512]{1,0:T(8,128)} fusion(bf16[8,30,512]{2,1,0:T(8,128)(2,1)S(1)} %copy.21, s32[]{:T(128)S(6)} %select_n.43, bf16[30,8,512]{2,0,1:T(8,128)(2,1)} %collective-permute-done, pred[]{:T(512)S(6)} %and.25, pred[]{:T(512)S(6)} %and.23), kind=kLoop, calls=%fused_computation.2 | loop fusion | flops 46080 | bytes 122886 | tf_op jit(solution)/shard_map/convert_element_type | solution.py:280
  68.9 25.8 %collective-permute-done.4.refs_0_ = bf16[4,2,96,512]{3,2,1,0:T(8,128)(2,1)S(1)} collective-permute-done((bf16[4,2,96,512]{3,2,1,0:T(8,128)(2,1)}, bf16[4,2,96,512]{3,2,1,0:T(8,128)(2,1)S(1)}, u32[]{:S(2)}, u32[]{:S(2)}) %collective-permute-start.4) | collective-permute-done | bytes 786464 | tf_op jit(solution)/shard_map/ppermute | solution.py:243
  94.8 1.0 copy-done.9
  95.7 1.5 %collective-permute-start.6 = (bf16[4,2,96,512]{3,2,1,0:T(8,128)(2,1)}, bf16[4,2,96,512]{3,2,1,0:T(8,128)(2,1)}, u32[]{:S(2)}, u32[]{:S(2)}) collective-permute-start(bf16[4,2,96,512]{3,2,1,0:T(8,128)(2,1)} %tie.7.refs_3_.refs_4_), channel_id=1, source_target_pairs={{0,1},{1,0},{2,3},{3,2},{4,5},{5,4},{6,7},{7,6},{8,9},{9,8},{10,11... | collective-permute-start | bytes 2359304 | tf_op jit(solution)/shard_map/ppermute | solution.py:243
  97.2 0.0 all-to-all-done.2
  97.2 0.6 slice.4.refs_1_
  97.9 0.0 collective-permute-done.5.refs_4_.refs_5_
  97.9 4.9 %all-to-all-start.3 = ((bf16[16,128,128]{2,1,0:T(8,128)(2,1)}), bf16[16,128,128]{2,1,0:T(8,128)(2,1)}, u32[]{:S(2)}, u32[]{:S(2)}) async-start(bf16[16,128,128]{2,1,0:T(8,128)(2,1)} %tie.8), calls=%async_computation.3 | async-start | bytes 1048576 | tf_op jit(solution)/shard_map/all_to_all | solution.py:363
  102.8 0.4 collective-permute-start.7
  103.2 0.2 collective-permute-start.8
  103.4 0.3 collective-permute-start.9
  103.7 9.1 %pool.1.refs_1_.pooled_ref = bf16[640,512]{1,0:T(8,128)(2,1)S(1)} custom-call(s32[8,1024]{1,0:T(8,128)S(1)} %get-tuple-element.7.place_ref, f32[8,1024]{1,0:T(8,128)S(1)} %bitcast.46, bf16[3072,128]{1,0:T(8,128)(2,1)S(1)} %bitcast.44, bf16[7168,128]{1,0:T(8,128)(2,1)S(1)} %bitcast.40), custom_call_target="tpu_custom_call" | custom-call | bytes 25165824 | tf_op jit(solution)/shard_map/pool/pallas_call | solution.py:366
  112.8 0.8 copy-done.4
  113.7 1.5 %collective-permute-done.6.refs_0_ = bf16[4,2,96,512]{3,2,1,0:T(8,128)(2,1)} collective-permute-done((bf16[4,2,96,512]{3,2,1,0:T(8,128)(2,1)}, bf16[4,2,96,512]{3,2,1,0:T(8,128)(2,1)}, u32[]{:S(2)}, u32[]{:S(2)}) %collective-permute-start.6) | collective-permute-done | bytes 786464 | tf_op jit(solution)/shard_map/ppermute | solution.py:243
  115.2 0.0 collective-permute-start.10
  115.2 0.6 pad_add_fusion.me_ref
  115.8 0.0 collective-permute-done.8.refs_8_
  115.8 1.9 %collective-permute-done.10.refs_10_ = bf16[4,2,96,512]{3,2,1,0:T(8,128)(2,1)S(1)} collective-permute-done((bf16[4,2,96,512]{3,2,1,0:T(8,128)(2,1)}, bf16[4,2,96,512]{3,2,1,0:T(8,128)(2,1)S(1)}, u32[]{:S(2)}, u32[]{:S(2)}) %collective-permute-start.10) | collective-permute-done | bytes 786464 | tf_op jit(solution)/shard_map/ppermute | solution.py:243
  117.6 0.0 all-to-all-done.3
  117.7 0.9 copy-done.17
  118.5 15.7 %stage.1 = bf16[1024,512]{1,0:T(8,128)(2,1)} custom-call(s32[8,1024]{1,0:T(8,128)} %copy-done.6, s32[2]{0:T(128)} %pad_add_fusion.me_ref, f32[8,1024]{1,0:T(8,128)} %bitcast.45, f32[30,512]{1,0:T(8,128)} %fusion.refs_1_.refs_2_.carried_ref, f32[4,512]{1,0:T(4,128)} %gain_ref.1, bf16[640,512]{1,0:T(8,128)(2,1)} %copy-done.4, bf16[3072,128]{1,0:T(8,128)(2,1)} %bitcast.43, ...), custom_call_target="tpu_custom_call" | custom-call | flops 6442450944 | bytes 25165824 | tf_op jit(solution)/shard_map/stage/pallas_call | solution.py:387
  (35 shorter events, 0.1 us)
Async XLA Ops:
  0.0 1.0 copy-start
  1.0 18.5 %collective-permute-start.2 = (bf16[2,96,512]{2,1,0:T(8,128)(2,1)S(1)}, bf16[2,96,512]{2,1,0:T(8,128)(2,1)S(1)}, u32[]{:S(2)}, u32[]{:S(2)}) collective-permute-start(bf16[2,96,512]{2,1,0:T(8,128)(2,1)S(1)} %constant_dynamic-slice_fusion), channel_id=1, source_target_pairs={{0,16},{2,18},{4,20},{6,22},{8,24},{10,26},{12,28},{14,30},{16,0},... | collective-permute-start | bytes 589832 | tf_op jit(solution)/shard_map/ppermute | solution.py:243
  5.1 14.4 %collective-permute-start.1 = (bf16[2,96,512]{2,1,0:T(8,128)(2,1)S(1)}, bf16[2,96,512]{2,1,0:T(8,128)(2,1)S(1)}, u32[]{:S(2)}, u32[]{:S(2)}) collective-permute-start(bf16[2,96,512]{2,1,0:T(8,128)(2,1)S(1)} %constant_dynamic-slice_fusion), channel_id=1, source_target_pairs={{0,8},{2,10},{4,12},{6,14},{8,0},{10,2},{12,4},{14,6},{16,24},{18,... | collective-permute-start | bytes 589832 | tf_op jit(solution)/shard_map/ppermute | solution.py:243
  6.7 0.8 copy-start.7
  7.5 0.8 copy-start.8
  9.5 94.3 %copy-start.6 = (s32[8,1024]{1,0:T(8,128)}, s32[8,1024]{1,0:T(8,128)S(1)}, u32[]{:S(2)}) copy-start(s32[8,1024]{1,0:T(8,128)S(1)} %get-tuple-element.7.place_ref) | copy-start | bytes 98308
  19.5 0.7 copy-start.10
  19.5 0.7 copy-start.14
  25.6 23.5 %all-to-all-start.1 = ((bf16[16,192,128]{2,1,0:T(8,128)(2,1)}), bf16[16,192,128]{2,1,0:T(8,128)(2,1)S(1)}, u32[]{:S(2)}, u32[]{:S(2)}) async-start(bf16[16,192,128]{2,1,0:T(8,128)(2,1)} %owner_gather.3.refs_0_), calls=%async_computation.1 | async-start | bytes 1572864 | tf_op jit(solution)/shard_map/all_to_all | solution.py:363
  29.3 19.9 %collective-permute-start.3 = (bf16[2,96,512]{2,1,0:T(8,128)(2,1)}, bf16[2,96,512]{2,1,0:T(8,128)(2,1)S(1)}, u32[]{:S(2)}, u32[]{:S(2)}) collective-permute-start(bf16[2,96,512]{2,1,0:T(8,128)(2,1)} %tie.5), channel_id=1, source_target_pairs={{0,8},{2,10},{4,12},{6,14},{8,0},{10,2},{12,4},{14,6},{16,24},{18,... | collective-permute-start | bytes 589832 | tf_op jit(solution)/shard_map/ppermute | solution.py:243
  49.2 0.7 copy-start.12
  49.2 1.0 copy-start.2
  50.1 5.0 %copy-start.11 = (bf16[2,96,512]{2,1,0:T(8,128)(2,1)S(1)}, bf16[2,96,512]{2,1,0:T(8,128)(2,1)}, u32[]{:S(2)}) copy-start(bf16[2,96,512]{2,1,0:T(8,128)(2,1)} %tie.5) | copy-start | bytes 589828
  50.1 5.0 %copy-start.13 = (bf16[2,96,512]{2,1,0:T(8,128)(2,1)S(1)}, bf16[2,96,512]{2,1,0:T(8,128)(2,1)}, u32[]{:S(2)}) copy-start(bf16[2,96,512]{2,1,0:T(8,128)(2,1)} %copy-done.12) | copy-start | bytes 589828
  50.2 5.0 %copy-start.15 = (bf16[2,96,512]{2,1,0:T(8,128)(2,1)S(1)}, bf16[2,96,512]{2,1,0:T(8,128)(2,1)}, u32[]{:S(2)}) copy-start(bf16[2,96,512]{2,1,0:T(8,128)(2,1)} %copy-done.14) | copy-start | bytes 589828
  50.2 47.1 %all-to-all-start.2 = ((bf16[16,448,128]{2,1,0:T(8,128)(2,1)}), bf16[16,448,128]{2,1,0:T(8,128)(2,1)S(1)}, u32[]{:S(2)}, u32[]{:S(2)}) async-start(bf16[16,448,128]{2,1,0:T(8,128)(2,1)} %tie.6), calls=%async_computation.2 | async-start | bytes 3670016 | tf_op jit(solution)/shard_map/all_to_all | solution.py:363
  55.1 3.0 %copy-start.16 = (bf16[8,30,512]{2,0,1:T(8,128)(2,1)S(1)}, bf16[8,30,512]{2,0,1:T(8,128)(2,1)}, u32[]{:S(2)}) copy-start(bf16[8,30,512]{2,0,1:T(8,128)(2,1)} %param.17) | copy-start | bytes 737284
  56.2 38.6 %collective-permute-start.4 = (bf16[4,2,96,512]{3,2,1,0:T(8,128)(2,1)}, bf16[4,2,96,512]{3,2,1,0:T(8,128)(2,1)S(1)}, u32[]{:S(2)}, u32[]{:S(2)}) collective-permute-start(bf16[4,2,96,512]{3,2,1,0:T(8,128)(2,1)} %pad_maximum_fusion.refs_3_), channel_id=1, source_target_pairs={{0,4},{2,6},{4,0},{6,2},{8,12},{10,14},{12,8},{14,10},{16,20},{18,... | collective-permute-start | bytes 2359304 | tf_op jit(solution)/shard_map/ppermute | solution.py:243
  58.2 9.4 %collective-permute-start = (bf16[30,8,512]{2,0,1:T(8,128)(2,1)S(1)}, bf16[30,8,512]{2,0,1:T(8,128)(2,1)}, u32[]{:S(2)}, u32[]{:S(2)}) collective-permute-start(bf16[30,8,512]{2,0,1:T(8,128)(2,1)S(1)} %bitcast.59), channel_id=1, source_target_pairs={{0,1},{1,0},{2,3},{3,2},{4,5},{5,4},{6,7},{7,6},{8,9},{9,8},{10,11... | collective-permute-start | bytes 737288 | tf_op jit(solution)/shard_map/ppermute | solution.py:276
  59.7 38.1 %collective-permute-start.5 = (bf16[4,2,96,512]{3,2,1,0:T(8,128)(2,1)}, bf16[4,2,96,512]{3,2,1,0:T(8,128)(2,1)}, u32[]{:S(2)}, u32[]{:S(2)}) collective-permute-start(bf16[4,2,96,512]{3,2,1,0:T(8,128)(2,1)} %pad_maximum_fusion.refs_3_), channel_id=1, source_target_pairs={{0,1},{1,0},{2,3},{3,2},{4,5},{5,4},{6,7},{7,6},{8,9},{9,8},{10,11... | collective-permute-start | bytes 2359304 | tf_op jit(solution)/shard_map/ppermute | solution.py:243
  94.8 1.0 copy-start.9
  95.7 19.4 %collective-permute-start.6 = (bf16[4,2,96,512]{3,2,1,0:T(8,128)(2,1)}, bf16[4,2,96,512]{3,2,1,0:T(8,128)(2,1)}, u32[]{:S(2)}, u32[]{:S(2)}) collective-permute-start(bf16[4,2,96,512]{3,2,1,0:T(8,128)(2,1)} %tie.7.refs_3_.refs_4_), channel_id=1, source_target_pairs={{0,1},{1,0},{2,3},{3,2},{4,5},{5,4},{6,7},{7,6},{8,9},{9,8},{10,11... | collective-permute-start | bytes 2359304 | tf_op jit(solution)/shard_map/ppermute | solution.py:243
  97.2 6.5 %copy-start.1 = (bf16[16,448,128]{2,1,0:T(8,128)(2,1)}, bf16[16,448,128]{2,1,0:T(8,128)(2,1)S(1)}, u32[]{:S(2)}) copy-start(bf16[16,448,128]{2,1,0:T(8,128)(2,1)S(1)} %all-to-all-done.2) | copy-start | bytes 5505028
  97.9 5.9 %copy-start.3 = (bf16[16,192,128]{2,1,0:T(8,128)(2,1)S(1)}, bf16[16,192,128]{2,1,0:T(8,128)(2,1)}, u32[]{:S(2)}) copy-start(bf16[16,192,128]{2,1,0:T(8,128)(2,1)} %copy-done.2) | copy-start | bytes 2359300
  97.9 5.9 %copy-start.5 = (f32[1,1024,8]{1,2,0:T(8,128)S(1)}, f32[1,1024,8]{1,2,0:T(8,128)}, u32[]{:S(2)}) copy-start(f32[1,1024,8]{1,2,0:T(8,128)} %param.12) | copy-start | bytes 98308
  97.9 19.8 %all-to-all-start.3 = ((bf16[16,128,128]{2,1,0:T(8,128)(2,1)}), bf16[16,128,128]{2,1,0:T(8,128)(2,1)}, u32[]{:S(2)}, u32[]{:S(2)}) async-start(bf16[16,128,128]{2,1,0:T(8,128)(2,1)} %tie.8), calls=%async_computation.3 | async-start | bytes 1048576 | tf_op jit(solution)/shard_map/all_to_all | solution.py:363
  102.8 12.9 %collective-permute-start.7 = (bf16[4,2,96,512]{3,2,1,0:T(8,128)(2,1)}, bf16[4,2,96,512]{3,2,1,0:T(8,128)(2,1)}, u32[]{:S(2)}, u32[]{:S(2)}) collective-permute-start(bf16[4,2,96,512]{3,2,1,0:T(8,128)(2,1)} %pad_maximum_fusion.refs_3_), channel_id=1, source_target_pairs={{0,2},{2,0},{4,6},{6,4},{8,10},{10,8},{12,14},{14,12},{16,18},{18,... | collective-permute-start | bytes 2359304 | tf_op jit(solution)/shard_map/ppermute | solution.py:243
  103.2 12.5 %collective-permute-start.8 = (bf16[4,2,96,512]{3,2,1,0:T(8,128)(2,1)}, bf16[4,2,96,512]{3,2,1,0:T(8,128)(2,1)}, u32[]{:S(2)}, u32[]{:S(2)}) collective-permute-start(bf16[4,2,96,512]{3,2,1,0:T(8,128)(2,1)} %tie.7.refs_3_.refs_4_), channel_id=1, source_target_pairs={{0,2},{2,0},{4,6},{6,4},{8,10},{10,8},{12,14},{14,12},{16,18},{18,... | collective-permute-start | bytes 2359304 | tf_op jit(solution)/shard_map/ppermute | solution.py:243
  103.4 12.4 %collective-permute-start.9 = (bf16[4,2,96,512]{3,2,1,0:T(8,128)(2,1)}, bf16[4,2,96,512]{3,2,1,0:T(8,128)(2,1)}, u32[]{:S(2)}, u32[]{:S(2)}) collective-permute-start(bf16[4,2,96,512]{3,2,1,0:T(8,128)(2,1)} %collective-permute-done.5.refs_4_.refs_5_), channel_id=1, source_target_pairs={{0,2},{2,0},{4,6},{6,4},{8,10},{10,8},{12,14},{14,12},{16,18},{18,... | collective-permute-start | bytes 2359304 | tf_op jit(solution)/shard_map/ppermute | solution.py:243
  112.8 0.8 copy-start.4
  115.2 2.5 %collective-permute-start.10 = (bf16[4,2,96,512]{3,2,1,0:T(8,128)(2,1)}, bf16[4,2,96,512]{3,2,1,0:T(8,128)(2,1)S(1)}, u32[]{:S(2)}, u32[]{:S(2)}) collective-permute-start(bf16[4,2,96,512]{3,2,1,0:T(8,128)(2,1)} %tie.9.refs_6_), channel_id=1, source_target_pairs={{0,2},{2,0},{4,6},{6,4},{8,10},{10,8},{12,14},{14,12},{16,18},{18,... | collective-permute-start | bytes 2359304 | tf_op jit(solution)/shard_map/ppermute | solution.py:243
  117.6 0.9 copy-start.17
